TPU v7x, 256 devices: a whole 4x4x8 slice. The times are simulated.
256 devices in a mesh: tile: 2 (over core), pts: 16 (over y, x), grp: 8 (over z).
Axes of the slice: x: 4, y: 4, z: 8, core: 2. Of those that a mesh axis runs over, the one named last changes fastest.
Arguments:
- lidar_features: bfloat16 [262144, 128], P(('tile', 'pts', 'grp')), parts along dimension 0, may hold values from -6 to 6
- reorder_targets: int32 [1, 262144], P(None, ('tile', 'pts', 'grp')), parts along dimension 1, may hold values from 0 to 131071, as said below
- adjacency_targets: int32 [1, 27, 262144], P(None, None, ('tile', 'pts', 'grp')), parts along dimension 2, may hold values from -1 to 131071, as said below
- spatial_stencil_coefficients: bfloat16 [1, 27, 128, 128], replicated, may hold values from -0.15625 to 0.15625
- triple_lens_coefficients: bfloat16 [1, 128, 384], replicated, may hold values from -0.5 to 0.5
- logit_sharpness: float32 [1, 8], replicated, may hold values from 2 to 12
- mixer_exit_coefficients: bfloat16 [1, 128, 128], replicated, may hold values from -0.5 to 0.5
- film_coefficients: float32 [512], P('tile'), parts along dimension 0, may hold values from -3 to 3
- widening_coefficients: bfloat16 [1, 128, 512], replicated, may hold values from -0.5 to 0.5
- narrowing_coefficients: bfloat16 [1, 512, 128], replicated, may hold values from -0.25 to 0.25
Outputs:
- features: bfloat16 [262144, 128], P(('tile', 'pts', 'grp')), parts along dimension 0
There are 2 independent parts, one for each index of `tile`. A program takes and returns all parts, laid end to end along the dimension named above; an argument that names none is the same for every part. Nothing has to cross between parts.
Inputs may be any that keep to these rules, and one draw needn't show every extreme that they name: `reorder_targets`: each block's row is a permutation of 0 to 131071. The 1024 rows of one device send at most 16 points to any one device's rows, and exactly 16 to some device. `adjacency_targets`: entry t = 13 is the point itself; every other present neighbour lies within 128 positions of the point in the new order.
All inputs are finite; a program needn't handle non-finite values.
Results may differ from a plain program's by a relative error of at most 0.0065.
Values may be sent and summed in bfloat16 or wider, within the bound.
A program may use at most 64 MiB of HBM per device.

v0:
```python
import jax
import jax.numpy as jnp
from jax import lax
from jax.sharding import PartitionSpec as P

PATCH = 1024
HALO = 128
LAYER_TOTAL = 1


def extended_2(array, sides, width):
    for axis, dim in sides:
        size, length = (lax.axis_size(axis), array.shape[dim])
        up = [(i, (i + 1) % size) for i in range(size - 1)]
        down = [(j, i) for i, j in up]
        last = lax.slice_in_dim(array, length - width, length, axis=dim)
        initial = lax.slice_in_dim(array, 0, width, axis=dim)
        before = lax.ppermute(last, axis, up)
        after = lax.ppermute(initial, axis, down)
        array = jnp.concatenate([before, array, after], axis=dim)
    return array


def normalize(values):
    average = jnp.mean(values, axis=-1, keepdims=True)
    centred = values - average
    spread = jnp.mean(centred * centred, axis=-1, keepdims=True)
    return centred * lax.rsqrt(spread + 1e-05)


def unit_heads(block_vals, focus_total):
    shaped = block_vals.reshape(block_vals.shape[0], focus_total, -1)
    power = jnp.mean(shaped * shaped, axis=-1, keepdims=True)
    return (shaped * lax.rsqrt(jnp.maximum(power, 0.25))).astype(jnp.bfloat16)


def patch_group(
    patch_entries,
    gathered_entries,
    stencil_coefficients,
    triple_lens_local,
    logit_sharpness_local,
    mixer_exit_coefficients_local,
    film_gain_vector,
    film_bias_vector,
    widen_coefficients,
    shrink_coefficients,
):
    channels = patch_entries.shape[1]
    convolved = lax.dot_general(
        gathered_entries,
        stencil_coefficients,
        (((0, 2), (0, 1)), ((), ())),
        preferred_element_type=jnp.float32,
    )
    after_conv = patch_entries.astype(jnp.float32) + normalize(convolved)
    normed = normalize(after_conv).astype(jnp.bfloat16)
    projected = jnp.dot(normed, triple_lens_local, preferred_element_type=jnp.float32)
    focus_total = logit_sharpness_local.shape[0]
    focus_breadth = channels // focus_total
    unit_queries = unit_heads(projected[:, :channels], focus_total)
    unit_keys = unit_heads(projected[:, channels : 2 * channels], focus_total)
    values = (
        projected[:, 2 * channels :].reshape(-1, focus_total, focus_breadth).astype(jnp.bfloat16)
    )
    head_outputs = []
    for focus_ordinal in range(focus_total):
        affinity_logits = lax.dot_general(
            unit_queries[:, focus_ordinal],
            unit_keys[:, focus_ordinal],
            (((1,), (1,)), ((), ())),
            preferred_element_type=jnp.float32,
        )
        affinity_logits = affinity_logits * (logit_sharpness_local[focus_ordinal] / focus_breadth)
        expo = jnp.exp(affinity_logits)
        totals = jnp.sum(expo, axis=-1, keepdims=True)
        weighted = jnp.dot(
            expo.astype(jnp.bfloat16), values[:, focus_ordinal], preferred_element_type=jnp.float32
        )
        head_outputs.append(weighted / totals)
    mixed = jnp.concatenate(head_outputs, axis=-1).astype(jnp.bfloat16)
    after_attn = after_conv + jnp.dot(
        mixed, mixer_exit_coefficients_local, preferred_element_type=jnp.float32
    )
    film_input = (normalize(after_attn) * (1.0 + film_gain_vector) + film_bias_vector).astype(
        jnp.bfloat16
    )
    hidden = jax.nn.gelu(
        jnp.dot(film_input, widen_coefficients, preferred_element_type=jnp.float32),
        approximate=True,
    ).astype(jnp.bfloat16)
    after_mlp = after_attn + jnp.dot(
        hidden, shrink_coefficients, preferred_element_type=jnp.float32
    )
    return after_mlp.astype(jnp.bfloat16)


def pack_slots(stream, dest, place, valid, device_count, capacity, dump_row):
    rows_dev = stream.shape[0]
    sort_key = jnp.where(valid, dest, device_count)
    ordering = jnp.argsort(sort_key)
    owner_ids = jnp.arange(device_count, dtype=jnp.int32)
    counts = jnp.sum((sort_key[:, None] == owner_ids[None, :]).astype(jnp.int32), axis=0)
    firsts = jnp.cumsum(counts) - counts
    lane_ids = jnp.arange(capacity, dtype=jnp.int32)
    filled = lane_ids[None, :] < counts[:, None]
    picked = ordering[jnp.minimum(firsts[:, None] + lane_ids[None, :], rows_dev - 1)]
    outgoing = jnp.where(filled[:, :, None], stream[picked], jnp.zeros((), jnp.bfloat16))
    places = jnp.where(filled, place[picked], dump_row)
    return (outgoing, places)


def send_slots(outgoing, places):
    channels = outgoing.shape[-1]
    arrived, landing = (
        lax.all_to_all(outgoing, ("pts", "grp"), split_axis=0, concat_axis=0, tiled=True),
        lax.all_to_all(places, ("pts", "grp"), split_axis=0, concat_axis=0, tiled=True),
    )
    return (arrived.reshape(-1, channels), landing.reshape(-1))


def reorder_with_rim(stream, targets, device_count, capacity):
    rows_dev, channels = stream.shape
    owners = targets // rows_dev
    slot_ids = targets % rows_dev
    every = jnp.ones_like(owners, dtype=bool)
    outgoing, places = pack_slots(stream, owners, slot_ids, every, device_count, capacity, rows_dev)
    arrived, landing = send_slots(outgoing, places)
    placed = jnp.zeros((rows_dev + 1, channels), jnp.bfloat16).at[landing].set(arrived)
    own_rows = placed[:rows_dev]
    extended = extended_2(own_rows, ((("pts", "grp"), 0),), HALO)
    return (own_rows, extended)


def shards(
    lidar_features,
    reorder_targets,
    adjacency_targets,
    spatial_stencil_coefficients,
    triple_lens_coefficients,
    logit_sharpness,
    mixer_exit_coefficients,
    film_coefficients,
    widening_coefficients,
    narrowing_coefficients,
):
    rows_dev, channels = lidar_features.shape
    device_count = lax.axis_size(("pts", "grp"))
    capacity = 2 * rows_dev // device_count
    film_layer_grid = film_coefficients.reshape(LAYER_TOTAL, 2, channels)
    first_global = lax.axis_index(("pts", "grp")) * rows_dev
    stream = lidar_features
    layer_ordinal = 0
    current, extended = reorder_with_rim(
        stream, reorder_targets[layer_ordinal], device_count, capacity
    )
    filled_entries = jnp.concatenate([extended, jnp.zeros((1, channels), jnp.bfloat16)], axis=0)
    gather_rows = jnp.where(
        adjacency_targets[layer_ordinal] < 0,
        rows_dev + 2 * HALO,
        adjacency_targets[layer_ordinal] - first_global + HALO,
    )

    def per_patch(
        first_row,
        current=current,
        filled_entries=filled_entries,
        gather_rows=gather_rows,
        layer_ordinal=layer_ordinal,
    ):
        return patch_group(
            current,
            filled_entries[gather_rows],
            spatial_stencil_coefficients[layer_ordinal],
            triple_lens_coefficients[layer_ordinal],
            logit_sharpness[layer_ordinal],
            mixer_exit_coefficients[layer_ordinal],
            film_layer_grid[layer_ordinal, 0],
            film_layer_grid[layer_ordinal, 1],
            widening_coefficients[layer_ordinal],
            narrowing_coefficients[layer_ordinal],
        )

    firsts = jnp.arange(rows_dev // PATCH, dtype=jnp.int32) * PATCH
    stream = lax.map(per_patch, firsts).reshape(rows_dev, channels)
    return stream


def solution(mesh):
    in_specs = (
        P(("tile", "pts", "grp"), None),
        P(None, ("tile", "pts", "grp")),
        P(None, None, ("tile", "pts", "grp")),
        P(),
        P(),
        P(),
        P(),
        P("tile"),
        P(),
        P(),
    )
    out_specs = P(("tile", "pts", "grp"), None)
    return jax.shard_map(shards, mesh=mesh, in_specs=in_specs, out_specs=out_specs, check_vma=False)
```

profile of v0, /device:TPU:8, one launch (start us, length us, event | category | flops | bytes accessed | tf_op | source)
XLA Modules:
  0.0 217.3 jit_solution(4037818207560300530)
XLA Ops:
  0.0 0.8 add_select_fusion.1
  0.8 0.2 convert_reduce_fusion
  1.0 4.4 %sort.17 = (s32[1024]{0:T(1024)}, s32[1024]{0:T(1024)S(1)}) sort(s32[1024]{0:T(1024)S(1)} %get-tuple-element.35, s32[1024]{0:T(1024)S(1)} %iota.21), dimensions={0}, to_apply=%region_1.2 | sort | flops 10240 | bytes 16384 | tf_op jit(solution)/shard_map/jit(argsort)/sort | solution.py:101
  5.4 0.1 copy.34
  5.5 0.2 reduce-window.8
  5.7 0.1 reduce
  5.8 0.1 compare_select_fusion.3
  5.9 0.1 reshape.366
  6.0 8.6 %gather_fusion = s32[2048]{0:T(1024)S(1)} fusion(s32[1024]{0:T(1024)S(1)} %get-tuple-element.28, s32[2048]{0:T(1024)S(1)} %broadcast_clamp_fusion.1), kind=kCustom, calls=%fused_computation | custom fusion | bytes 24576 | tf_op jit(solution)/shard_map/gather | solution.py:107
  14.6 0.1 gather.18
  14.7 0.1 reshape.374
  14.8 8.6 %gather_fusion.1 = s32[2048]{0:T(1024)S(1)} fusion(s32[1024]{0:T(1024)S(1)} %get-tuple-element.48, s32[2048]{0:T(1024)S(1)} %broadcast_clamp_fusion.2), kind=kCustom, calls=%fused_computation.1 | custom fusion | bytes 24576 | tf_op jit(solution)/shard_map/gather | solution.py:109
  23.3 0.0 copy-start.2
  23.4 0.1 gather.20
  23.5 0.7 fusion.146
  24.2 15.4 %all-to-all-start = ((s32[128,1,16]{2,1,0:T(1,128)}), s32[128,1,16]{2,1,0:T(1,128)S(1)}, u32[]{:S(2)}, u32[]{:S(2)}) async-start(s32[128,1,16]{2,1,0:T(1,128)} %bitcast.2), calls=%async_computation | async-start | bytes 131072 | tf_op jit(solution)/shard_map/all_to_all | solution.py:117
  39.6 0.1 iota_compare_fusion.1
  39.7 6.2 %gather_fusion.2 = bf16[2048,128]{1,0:T(8,128)(2,1)S(1)} fusion(bf16[1024,128]{1,0:T(8,128)(2,1)S(1)} %copy-done.1, s32[2048]{0:T(1024)S(1)} %broadcast_clamp_fusion.2), kind=kCustom, calls=%fused_computation.2 | custom fusion | bytes 1056768 | tf_op jit(solution)/shard_map/gather | solution.py:108
  45.9 1.1 broadcast_select_fusion
  47.1 0.2 compare_select_fusion
  47.3 3.1 %all-to-all-done = s32[128,1,16]{2,1,0:T(1,128)S(1)} async-done(((s32[128,1,16]{2,1,0:T(1,128)}), s32[128,1,16]{2,1,0:T(1,128)S(1)}, u32[]{:S(2)}, u32[]{:S(2)}) %all-to-all-start) | async-done | bytes 8224 | tf_op jit(solution)/shard_map/all_to_all | solution.py:117
  50.4 10.7 %all-to-all-start.1 = ((bf16[128,16,128]{2,1,0:T(8,128)(2,1)}), bf16[128,16,128]{2,1,0:T(8,128)(2,1)S(1)}, u32[]{:S(2)}, u32[]{:S(2)}) async-start(bf16[128,16,128]{2,1,0:T(8,128)(2,1)} %broadcast_select_fusion), calls=%async_computation.1 | async-start | bytes 1048576 | tf_op jit(solution)/shard_map/all_to_all | solution.py:116
  61.2 0.5 broadcast.415
  61.7 0.8 reduce.4
  62.5 0.1 reshape.359
  62.6 16.2 %all-to-all-done.1 = bf16[128,16,128]{2,1,0:T(8,128)(2,1)S(1)} async-done(((bf16[128,16,128]{2,1,0:T(8,128)(2,1)}), bf16[128,16,128]{2,1,0:T(8,128)(2,1)S(1)}, u32[]{:S(2)}, u32[]{:S(2)}) %all-to-all-start.1) | async-done | bytes 524320 | tf_op jit(solution)/shard_map/all_to_all | solution.py:116
  78.8 5.8 %scatter_custom_fusion = bf16[1025,128]{1,0:T(8,128)(2,1)S(1)} fusion(s32[2048]{0:T(1024)S(1)} %bitcast.178, bf16[2048,128]{1,0:T(8,128)(2,1)S(1)} %bitcast.175, bf16[]{:T(256)} %constant.100.clone.1), kind=kCustom, calls=%fused_computation.114 | custom fusion | bytes 262402 | tf_op jit(solution)/shard_map/scatter | solution.py:129
  84.6 0.1 copy.47
  84.7 4.9 %collective-permute-start.1 = (bf16[128,128]{0,1:T(8,128)(2,1)S(1)}, bf16[128,128]{0,1:T(8,128)(2,1)S(1)}, u32[]{:S(2)}, u32[]{:S(2)}) collective-permute-start(bf16[128,128]{0,1:T(8,128)(2,1)S(1)} %copy.47), channel_id=1, source_target_pairs={{1,0},{2,1},{3,2},{4,3},{5,4},{6,5},{7,6},{8,7},{9,8},{10,9},{11,1... | collective-permute-start | bytes 98312 | tf_op jit(solution)/shard_map/ppermute | solution.py:19
  89.6 0.1 copy.46
  89.7 1.9 collective-permute-start
  91.6 0.7 fusion.164
  97.3 0.1 copy.45
  97.5 2.2 %collective-permute-done = bf16[128,128]{0,1:T(8,128)(2,1)S(1)} collective-permute-done((bf16[128,128]{0,1:T(8,128)(2,1)S(1)}, bf16[128,128]{0,1:T(8,128)(2,1)S(1)}, u32[]{:S(2)}, u32[]{:S(2)}) %collective-permute-start) | collective-permute-done | bytes 32800 | tf_op jit(solution)/shard_map/ppermute | solution.py:18
  99.7 0.1 maximum_maximum_fusion
  99.8 0.2 copy.39
  100.0 96.4 %gather_fusion.3 = bf16[27648,128]{1,0:T(8,128)(2,1)} fusion(bf16[1281,128]{1,0:T(8,128)(2,1)S(1)} %copy.39, s32[27648]{0:T(1024)S(1)} %broadcast_clamp_fusion), kind=kCustom, calls=%fused_computation.3 | custom fusion | bytes 14266368 | tf_op jit(solution)/shard_map/while/body/eval_jaxpr/gather | solution.py:173
  196.4 5.5 %fusion.165 = (f32[1024]{0:T(1024)S(1)}, f32[1024,128]{0,1:T(8,128)S(1)}) fusion(bf16[27,1024,128]{2,1,0:T(8,128)(2,1)} %bitcast.165, bf16[1,27,128,128]{3,2,1,0:T(8,128)(2,1)S(1)} %copy-done), kind=kOutput, calls=%fused_computation.185 | convolution fusion | flops 906099712 | bytes 8491008 | tf_op jit(solution)/shard_map/while/body/eval_jaxpr/dot_general | solution.py:50
  201.9 0.1 multiply_reduce_fusion.4
  202.0 0.1 fusion.162
  202.1 0.1 multiply_reduce_fusion.3
  202.3 0.4 fusion.128
  202.7 0.2 multiply_reduce_fusion.2
  203.0 0.1 multiply_convert_fusion.1
  203.1 0.8 fusion
  203.9 0.8 fusion.2
  204.7 0.8 fusion.4
  205.5 0.8 fusion.6
  206.3 0.8 fusion.8
  207.1 0.8 fusion.10
  207.9 0.8 fusion.12
  208.7 0.8 fusion.14
  209.5 0.7 fusion.120
  210.2 0.7 fusion.114
  210.8 0.7 fusion.108
  211.5 0.7 fusion.102
  212.2 0.7 fusion.96
  212.8 0.7 fusion.90
  213.5 0.7 fusion.84
  214.2 0.7 fusion.78
  214.9 0.3 fusion.166
  215.2 0.1 multiply_reduce_fusion
  215.3 1.1 fusion.50
  216.4 0.8 copy.42
  (37 shorter events, 0.2 us)
Async XLA Ops:
  0.0 196.4 %copy-start = (bf16[1,27,128,128]{3,2,1,0:T(8,128)(2,1)S(1)}, bf16[1,27,128,128]{3,2,1,0:T(8,128)(2,1)}, u32[]{:S(2)}) copy-start(bf16[1,27,128,128]{3,2,1,0:T(8,128)(2,1)} %param.13) | copy-start | bytes 2654212
  14.7 25.0 %copy-start.1 = (bf16[1024,128]{1,0:T(8,128)(2,1)S(1)}, bf16[1024,128]{1,0:T(8,128)(2,1)}, u32[]{:S(2)}) copy-start(bf16[1024,128]{1,0:T(8,128)(2,1)} %param.10) | copy-start | bytes 786436
  23.3 23.7 %copy-start.2 = (s32[1,27,1024]{2,0,1:T(1,128)S(1)}, s32[1,27,1024]{2,0,1:T(1,128)}, u32[]{:S(2)}) copy-start(s32[1,27,1024]{2,0,1:T(1,128)} %param.12) | copy-start | bytes 331780
  23.4 23.9 %copy-start.6 = (f32[256]{0:T(256)S(1)}, f32[256]{0:T(256)}, u32[]{:S(2)}) copy-start(f32[256]{0:T(256)} %param.17) | copy-start | bytes 3076
  23.5 68.1 %copy-start.5 = (f32[1,8]{1,0:T(1,128)S(1)}, f32[1,8]{1,0:T(1,128)}, u32[]{:S(2)}) copy-start(f32[1,8]{1,0:T(1,128)} %param.15) | copy-start | bytes 100
  24.2 26.2 %all-to-all-start = ((s32[128,1,16]{2,1,0:T(1,128)}), s32[128,1,16]{2,1,0:T(1,128)S(1)}, u32[]{:S(2)}, u32[]{:S(2)}) async-start(s32[128,1,16]{2,1,0:T(1,128)} %bitcast.2), calls=%async_computation | async-start | bytes 131072 | tf_op jit(solution)/shard_map/all_to_all | solution.py:117
  50.4 28.4 %all-to-all-start.1 = ((bf16[128,16,128]{2,1,0:T(8,128)(2,1)}), bf16[128,16,128]{2,1,0:T(8,128)(2,1)S(1)}, u32[]{:S(2)}, u32[]{:S(2)}) async-start(bf16[128,16,128]{2,1,0:T(8,128)(2,1)} %broadcast_select_fusion), calls=%async_computation.1 | async-start | bytes 1048576 | tf_op jit(solution)/shard_map/all_to_all | solution.py:116
  84.7 12.8 %collective-permute-start.1 = (bf16[128,128]{0,1:T(8,128)(2,1)S(1)}, bf16[128,128]{0,1:T(8,128)(2,1)S(1)}, u32[]{:S(2)}, u32[]{:S(2)}) collective-permute-start(bf16[128,128]{0,1:T(8,128)(2,1)S(1)} %copy.47), channel_id=1, source_target_pairs={{1,0},{2,1},{3,2},{4,3},{5,4},{6,5},{7,6},{8,7},{9,8},{10,9},{11,1... | collective-permute-start | bytes 98312 | tf_op jit(solution)/shard_map/ppermute | solution.py:19
  89.7 10.0 %collective-permute-start = (bf16[128,128]{0,1:T(8,128)(2,1)S(1)}, bf16[128,128]{0,1:T(8,128)(2,1)S(1)}, u32[]{:S(2)}, u32[]{:S(2)}) collective-permute-start(bf16[128,128]{0,1:T(8,128)(2,1)S(1)} %copy.46), channel_id=1, source_target_pairs={{0,1},{1,2},{2,3},{3,4},{4,5},{5,6},{6,7},{7,8},{8,9},{9,10},{10,1... | collective-permute-start | bytes 98312 | tf_op jit(solution)/shard_map/ppermute | solution.py:18
  196.4 5.9 %copy-start.3 = (bf16[1,128,384]{2,1,0:T(8,128)(2,1)S(1)}, bf16[1,128,384]{2,1,0:T(8,128)(2,1)}, u32[]{:S(2)}) copy-start(bf16[1,128,384]{2,1,0:T(8,128)(2,1)} %param.14) | copy-start | bytes 294916
  213.5 1.4 copy-start.4
  214.2 1.1 copy-start.7
  214.2 1.1 copy-start.8
where the time goes:
time: 218 us; the launch traced here: 217 us
  local copies, waits for them, and re-layouts  129 us (59%)
  starting transfers between devices  33 us (15%)
  waiting for transfers between devices  21.5 us (10%)
  matrix products  19 us (9%)
  other arithmetic  9.54 us (4%)
  between operations  5.43 us (2%)
    gather x1, local copies, waits for them, and re-layouts, per_patch(): filled_entries[gather_rows]  96.4 us
    all_to_all x1, waiting for transfers between devices, send_slots(): lax.all_to_all(outgoing, ('pts', 'grp'), split_axis=0, concat_axis=0, til...  16.2 us
    all_to_all x1, starting transfers between devices, send_slots(): lax.all_to_all(places, ('pts', 'grp'), split_axis=0, concat_axis=0, tiled...  15.4 us
    all_to_all x1, starting transfers between devices, send_slots(): lax.all_to_all(outgoing, ('pts', 'grp'), split_axis=0, concat_axis=0, til...  10.7 us
    gather x2, local copies, waits for them, and re-layouts, pack_slots(): places = jnp.where(filled, place[picked], dump_row)  8.66 us
    gather x2, local copies, waits for them, and re-layouts, pack_slots(): ordering[jnp.minimum(firsts[:, None] + lane_ids[None, :], rows_dev - 1)]  8.66 us
    dot_general x8, matrix products, patch_group(): lax.dot_general(unit_queries[:, focus_ordinal], unit_keys[:, focus_ordina...  6.33 us
    gather x1, local copies, waits for them, and re-layouts, pack_slots(): stream[picked]  6.19 us
  transfers between devices with their start and end apart: 4, of which 3 were waited for; matrix products, arithmetic and copies ran while one was open for 5% of the time, Pallas kernels for 0%

commit v1 on v0

v1 whole, which is shorter than its diff:
```python
import functools

import jax
import jax.numpy as jnp
from jax import lax
from jax.experimental import pallas as pl
from jax.experimental.pallas import tpu as pltpu
from jax.sharding import PartitionSpec as P

MESH = pl.DeviceIdType.MESH
F32, BF16, I32 = jnp.float32, jnp.bfloat16, jnp.int32
ROWS = 1024
C = 128
HALO = 128
HEADS = 8
TAPS = 27
EXT = ROWS + 2 * HALO
BLK = 256
LOG2E = 1.4426950408889634


def dot(a, b):
    return jnp.dot(a, b, preferred_element_type=F32)


def dot_nt(a, b):
    return lax.dot_general(a, b, (((1,), (1,)), ((), ())), preferred_element_type=F32)


def onehot(mask):
    return jnp.where(mask, 1.0, 0.0).astype(BF16)


def iota(shape, dim):
    return lax.broadcasted_iota(I32, shape, dim)


def z_peer(dz):
    return (lax.axis_index("tile"), lax.axis_index("pts"), (lax.axis_index("grp") + dz) & 7)


def xy_peer(half, idx):
    me = lax.axis_index("pts")
    dy = idx >> 1
    dx = 2 * (idx & 1) + ((half + dy) & 1)
    return (
        lax.axis_index("tile"),
        (((me >> 2) + dy) & 3) * 4 + (((me & 3) + dx) & 3),
        lax.axis_index("grp"),
    )


def slab_peer(step):
    me = (lax.axis_index("pts") * 8 + lax.axis_index("grp") + step) & 127
    return (lax.axis_index("tile"), me >> 3, me & 7)


def reorder_kernel(
    x_ref, target_ref, ext_ref, send, mid, land, msend, mmid, mland, rim, ssem, rsem, hsem
):
    pts, grp = lax.axis_index("pts"), lax.axis_index("grp")
    peers = [z_peer(i) for i in range(1, 8)]
    peers += [xy_peer(0, i) for i in range(1, 8)] + [xy_peer(1, i) for i in range(8)]
    peers += [slab_peer(1), slab_peer(-1)]
    barrier = pltpu.get_barrier_semaphore()
    for peer in peers:
        pl.semaphore_signal(barrier, inc=1, device_id=peer, device_id_type=MESH)

    target = target_ref[...]
    owner = target >> 10
    dy = ((owner >> 5) - (pts >> 2)) & 3
    dx = ((owner >> 3) - (pts & 3)) & 3
    dz = (owner - grp) & 7
    flat = dy * 2 + (dx >> 1)
    group = jnp.where(((dx + dy) & 1) == 0, dz * 8 + flat, 64 + flat * 8 + dz)
    member = iota((128, ROWS), 0) == group
    member_bf = onehot(member)
    earlier = onehot(iota((BLK, BLK), 0) < iota((BLK, BLK), 1))
    carry = jnp.zeros((128, 1), F32)
    ranks = []
    for b in range(ROWS // BLK):
        cols = slice(b * BLK, (b + 1) * BLK)
        part = member_bf[:, cols]
        count = dot(part, earlier) + carry
        ranks.append(jnp.sum(jnp.where(member[:, cols], count, 0.0), axis=0, keepdims=True))
        if b < ROWS // BLK - 1:
            carry = carry + jnp.sum(part.astype(F32), axis=1, keepdims=True)
    rank = jnp.concatenate(ranks, axis=1).astype(I32)
    slot = group * 16 + rank
    lane = ((group >> 3) & 7) * 16 + rank
    place = (target & 1023) + 1
    here = iota((128, ROWS), 0) == lane
    high = jnp.where(here, (place >> 5).astype(F32), 0.0).astype(BF16)
    low = jnp.where(here, (place & 31).astype(F32), 0.0).astype(BF16)
    meta = (32.0 * dot_nt(member_bf, high) + dot_nt(member_bf, low)).reshape(16, 8, 128)
    msend[...] = meta
    mmid[0] = meta[0]

    pl.semaphore_wait(barrier, len(peers))

    def remote(kind, stage, idx, src, dst, peer):
        return pltpu.make_async_remote_copy(
            src, dst, ssem.at[kind, stage, idx], rsem.at[kind, stage, idx],
            device_id=peer, device_id_type=MESH,
        )

    def stage_copies(kind, one, two, three):
        first = [remote(kind, 0, i, one.at[i], two.at[i], z_peer(i)) for i in range(1, 8)]
        second = [remote(kind, 1, i, one.at[8 + i], two.at[8 + i], xy_peer(1, i)) for i in range(8)]
        third = [
            remote(kind, 2, i, two.at[0:8, i], three.at[i], xy_peer(0, i)) for i in range(1, 8)
        ]
        fourth = [
            remote(kind, 3, i, two.at[8:16, i], three.at[8 + i], z_peer(i)) for i in range(1, 8)
        ]
        return first, second, third, fourth

    meta_copies = stage_copies(0, msend, mmid, mland)
    data_copies = stage_copies(1, send, mid, land)

    def start(copies):
        for copy in copies:
            copy.start()

    def arrived(copies):
        for copy in copies:
            copy.wait_recv()

    start(meta_copies[0])
    start(meta_copies[1])
    x = x_ref[...]

    def pack(m0):
        hit = onehot(iota((512, ROWS), 0) + m0 * 128 == slot)
        return dot(hit, x).astype(BF16).reshape(4, 8, 16, C)

    for m0 in (8, 12):
        send[m0 : m0 + 4] = pack(m0)
        start(data_copies[1][m0 - 8 : m0 - 4])
    packed = pack(0)
    send[0:4] = packed
    mid[0] = packed[0]
    start(data_copies[0][0:3])
    send[4:8] = pack(4)
    start(data_copies[0][3:7])

    arrived(meta_copies[0])
    start(meta_copies[2])
    mland[0] = mmid[0:8, 0]
    arrived(meta_copies[1])
    start(meta_copies[3])
    mland[8] = mmid[8:16, 0]
    arrived(data_copies[1])
    start(data_copies[3])
    land[8] = mid[8:16, 0]
    arrived(data_copies[0])
    start(data_copies[2])
    land[0] = mid[0:8, 0]
    arrived(meta_copies[2])
    arrived(meta_copies[3])
    places = jnp.sum(mland[...], axis=1)

    def unpack(m0):
        total = jnp.zeros((ROWS, C), F32)
        for m in range(m0, m0 + 8, 2):
            want = jnp.concatenate([places[m : m + 1], places[m + 1 : m + 2]], axis=1)
            hit = onehot((iota((ROWS, 256), 0) + 1).astype(F32) == want)
            total = total + dot(hit, land[m : m + 2].reshape(256, C))
        return total

    arrived(data_copies[2])
    own = unpack(0)
    arrived(data_copies[3])
    own = (own + unpack(8)).astype(BF16)
    ext_ref[HALO : HALO + ROWS] = own
    rim[0] = own[:HALO]
    rim[1] = own[ROWS - HALO :]
    down = pltpu.make_async_remote_copy(
        rim.at[0], rim.at[2], hsem.at[0], hsem.at[1], device_id=slab_peer(-1), device_id_type=MESH
    )
    up = pltpu.make_async_remote_copy(
        rim.at[1], rim.at[3], hsem.at[2], hsem.at[3], device_id=slab_peer(1), device_id_type=MESH
    )
    down.start()
    up.start()
    for copies in meta_copies + data_copies:
        for copy in copies:
            copy.wait_send()
    up.wait()
    ext_ref[0:HALO] = rim[3]
    down.wait()
    ext_ref[HALO + ROWS :] = rim[2]


def reorder(x, target):
    vmem = pl.BlockSpec(memory_space=pltpu.VMEM)
    return pl.pallas_call(
        reorder_kernel,
        out_shape=jax.ShapeDtypeStruct((EXT, C), BF16),
        in_specs=[vmem, vmem],
        out_specs=vmem,
        scratch_shapes=[pltpu.VMEM((16, 8, 16, C), BF16)] * 3
        + [pltpu.VMEM((16, 8, 128), F32)] * 3
        + [
            pltpu.VMEM((4, HALO, C), BF16),
            pltpu.SemaphoreType.DMA((2, 4, 8)),
            pltpu.SemaphoreType.DMA((2, 4, 8)),
            pltpu.SemaphoreType.DMA((4,)),
        ],
        compiler_params=pltpu.CompilerParams(
            collective_id=0, has_side_effects=True, vmem_limit_bytes=48 << 20
        ),
    )(x, target)


def normalize(values):
    average = jnp.mean(values, axis=-1, keepdims=True)
    centred = values - average
    spread = jnp.mean(centred * centred, axis=-1, keepdims=True)
    return centred * lax.rsqrt(spread + 1e-05)


def head_power(values, spread):
    squares = values * values
    top = squares.astype(BF16)
    rest = (squares - top.astype(F32)).astype(BF16)
    return dot(jnp.concatenate([top, rest], axis=1), spread)


def block_kernel(
    ext_ref, adj_ref, stencil_ref, lens_ref, sharp_ref, mixer_ref, film_ref, wide_ref, narrow_ref,
    out_ref, hits, sides, gathered, conv, queries, keys, vals, mixed,
):
    first = (lax.axis_index("pts") * 8 + lax.axis_index("grp")) * ROWS
    lanes = iota((BLK, BLK), 1)
    for b in range(ROWS // BLK):
        rows = slice(b * BLK, (b + 1) * BLK)
        adj = adj_ref[:, rows]
        rel = jnp.where(adj < 0, -1, adj - (first + b * BLK - HALO))
        rel = jnp.concatenate([rel, jnp.full((32 - TAPS, BLK), -1, I32)], axis=0)
        rel = jnp.transpose(rel.astype(F32), (1, 0)).astype(I32)
        for t in range(TAPS):
            col = rel[:, t : t + 1]
            near = jnp.where(col < 0, -1, col & 255)
            hits[t, rows] = onehot(lanes == near)
            sides[t, rows] = onehot(jnp.broadcast_to(col >= 256, (BLK, C)))
    for b in range(ROWS // BLK):
        rows = slice(b * BLK, (b + 1) * BLK)
        pair = jnp.concatenate(
            [ext_ref[b * BLK : (b + 1) * BLK], ext_ref[(b + 1) * BLK : (b + 2) * BLK]], axis=1
        )
        for t in range(TAPS):
            both = dot(hits[t, rows], pair).astype(BF16)
            gathered[rows, t * C : (t + 1) * C] = jnp.where(
                sides[t, rows] > 0.5, both[:, C:], both[:, :C]
            )
        conv[rows] = dot(gathered[rows], stencil_ref[...])
    after_conv = ext_ref[HALO : HALO + ROWS].astype(F32) + normalize(conv[...])
    conv[...] = after_conv
    normed = normalize(after_conv).astype(BF16)
    projected = dot(normed, lens_ref[...])
    same = (iota((2 * C, C), 0) & 127) >> 4 == iota((2 * C, C), 1) >> 4
    spread = jnp.where(same, 1.0 / 16, 0.0).astype(BF16)
    q, k = projected[:, :C], projected[:, C : 2 * C]
    queries[...] = (q * lax.rsqrt(jnp.maximum(head_power(q, spread), 0.25))).astype(BF16)
    unit_keys = k * lax.rsqrt(jnp.maximum(head_power(k, spread), 0.25))
    keys[...] = jnp.transpose(unit_keys, (1, 0)).astype(BF16)
    values = projected[:, 2 * C :].astype(BF16)
    head_of = iota((ROWS, C), 1) >> 4
    for h in range(HEADS):
        vals[h] = jnp.concatenate(
            [jnp.where(head_of == h, values, jnp.zeros_like(values)), onehot(head_of == h)], axis=1
        )

    def attend(b, carry):
        rows = pl.ds(pl.multiple_of(b * BLK, BLK), BLK)
        q_blk = queries[rows]
        head = iota((BLK, C), 1) >> 4
        total = jnp.zeros((BLK, 2 * C), F32)
        for h in range(HEADS):
            q_head = jnp.where(head == h, q_blk, jnp.zeros_like(q_blk))
            scores = dot(q_head, keys[...]) * (sharp_ref[0, h] * (LOG2E / 16))
            total = total + dot(jnp.exp2(scores).astype(BF16), vals[h])
        mixed[rows] = (total[:, :C] / total[:, C:]).astype(BF16)
        return carry

    lax.fori_loop(0, ROWS // BLK, attend, 0)
    after_attn = conv[...] + dot(mixed[...], mixer_ref[...])
    film_input = (normalize(after_attn) * (1.0 + film_ref[0:1]) + film_ref[1:2]).astype(BF16)
    hidden = jax.nn.gelu(dot(film_input, wide_ref[...]), approximate=True).astype(BF16)
    out_ref[...] = (after_attn + dot(hidden, narrow_ref[...])).astype(BF16)


def block(ext, adjacency, stencil, lens, sharp, mixer, film, wide, narrow):
    vmem = pl.BlockSpec(memory_space=pltpu.VMEM)
    smem = pl.BlockSpec(memory_space=pltpu.SMEM)
    return pl.pallas_call(
        block_kernel,
        out_shape=jax.ShapeDtypeStruct((ROWS, C), BF16),
        in_specs=[vmem] * 4 + [smem] + [vmem] * 4,
        out_specs=vmem,
        scratch_shapes=[
            pltpu.VMEM((TAPS, ROWS, BLK), BF16),
            pltpu.VMEM((TAPS, ROWS, C), BF16),
            pltpu.VMEM((ROWS, TAPS * C), BF16),
            pltpu.VMEM((ROWS, C), F32),
            pltpu.VMEM((ROWS, C), BF16),
            pltpu.VMEM((C, ROWS), BF16),
            pltpu.VMEM((HEADS, ROWS, 2 * C), BF16),
            pltpu.VMEM((ROWS, C), BF16),
        ],
        compiler_params=pltpu.CompilerParams(vmem_limit_bytes=56 << 20),
    )(ext, adjacency, stencil, lens, sharp, mixer, film, wide, narrow)


def shards(features, targets, adjacency, stencil, lens, sharp, mixer, film, wide, narrow):
    ext = reorder(features, targets)
    return block(
        ext, adjacency[0], stencil[0].reshape(TAPS * C, C), lens[0], sharp, mixer[0],
        film.reshape(2, C), wide[0], narrow[0],
    )


def solution(mesh):
    rows = P(("tile", "pts", "grp"), None)
    in_specs = (
        rows,
        P(None, ("tile", "pts", "grp")),
        P(None, None, ("tile", "pts", "grp")),
        P(), P(), P(), P(), P("tile"), P(), P(),
    )
    return jax.shard_map(shards, mesh=mesh, in_specs=in_specs, out_specs=rows, check_vma=False)
```

time: 218 us -> 61.7 us (0.28)
  local copies, waits for them, and re-layouts: 129 us -> 3.25 us
  Pallas kernels: 0 us -> 58.3 us
  starting transfers between devices: 33 us -> 0 us
  waiting for transfers between devices: 21.5 us -> 0 us
  matrix products: 19 us -> 0 us
  other arithmetic: 9.54 us -> 0 us
  between operations: 5.43 us -> 0.02 us
    gather x6 -> x0, local copies, waits for them, and re-layouts: 120 us -> none  [the longest x1 96.4 us: per_patch(): filled_entries[gather_rows]]
    pallas_call x0 -> x2, Pallas kernels: none -> 58.3 us  [the longest x1 33.1 us: reorder(): pl.pallas_call(reorder_kernel, out_shape=jax.ShapeDtypeStruct((EXT, C), B...]
    all_to_all x2 -> x0, starting transfers between devices: 26.2 us -> none  [the longest x1 15.4 us: send_slots(): lax.all_to_all(places, ('pts', 'grp'), split_axis=0, concat_axis=0, tiled...]
    all_to_all x2 -> x0, waiting for transfers between devices: 19.3 us -> none  [the longest x1 16.2 us: send_slots(): lax.all_to_all(outgoing, ('pts', 'grp'), split_axis=0, concat_axis=0, til...]
    dot_general x20 -> x0, matrix products: 19 us -> none  [the longest x8 6.33 us: patch_group(): lax.dot_general(unit_queries[:, focus_ordinal], unit_keys[:, focus_ordina...]
    ppermute x2 -> x0, starting transfers between devices: 6.79 us -> none  [the longest x1 4.87 us: extended_2(): after = lax.ppermute(initial, axis, down)]
    scatter x1 -> x0, local copies, waits for them, and re-layouts: 5.76 us -> none  [reorder_with_rim(): jnp.zeros((rows_dev + 1, channels), jnp.bfloat16).at[landing].set(arrived)]
    sort x1 -> x0, other arithmetic: 4.37 us -> none  [pack_slots(): ordering = jnp.argsort(sort_key)]
  transfers between devices with their start and end apart: 4 -> 0, of which waited for: 3 -> 0; matrix products, arithmetic and copies ran while one was open for 5% -> 0% of each run, Pallas kernels for 0% -> 0%
where the time goes in v1:
time: 61.7 us; the launch traced here: 61.5 us
  Pallas kernels  58.3 us (94%)
  local copies, waits for them, and re-layouts  3.25 us (5%)
    pallas_call x1, Pallas kernels, reorder(): pl.pallas_call(reorder_kernel, out_shape=jax.ShapeDtypeStruct((EXT, C), B...  33.1 us
    pallas_call x1, Pallas kernels, block(): pl.pallas_call(block_kernel, out_shape=jax.ShapeDtypeStruct((ROWS, C), BF...  25.1 us
    unnamed x7, local copies, waits for them, and re-layouts  3.25 us

profile of v1, /device:TPU:8, one launch (start us, length us, event | category | flops | bytes accessed | tf_op | source)
XLA Modules:
  0.0 61.5 jit_solution(5245862904869424664)
XLA Ops:
  0.0 0.0 copy-start.2
  0.0 1.6 %copy.13 = s32[1,27,1024]{2,1,0:T(8,128)} copy(s32[1,27,1024]{2,0,1:T(1,128)} %param.12) | data formatting | bytes 221184
  1.6 0.0 copy-done.2
  1.6 0.0 copy-start.1
  1.6 0.9 %copy-done.1 = bf16[1024,128]{1,0:T(8,128)(2,1)S(1)} copy-done((bf16[1024,128]{1,0:T(8,128)(2,1)S(1)}, bf16[1024,128]{1,0:T(8,128)(2,1)}, u32[]{:S(2)}) %copy-start.1) | copy-done | bytes 262168
  2.5 33.1 %shard_map.100.ext_ref = bf16[1280,128]{1,0:T(8,128)(2,1)S(1)} custom-call(bf16[1024,128]{1,0:T(8,128)(2,1)S(1)} %copy-done.1, s32[1,1024]{1,0:T(1,128)S(1)} %copy-done.2), custom_call_target="tpu_custom_call" | custom-call | tf_op jit(solution)/shard_map/pallas_call | solution.py:197
  35.7 0.0 copy-start
  35.7 0.7 %copy-done = bf16[1280,128]{1,0:T(8,128)(2,1)} copy-done((bf16[1280,128]{1,0:T(8,128)(2,1)}, bf16[1280,128]{1,0:T(8,128)(2,1)S(1)}, u32[]{:S(2)}) %copy-start) | copy-done | bytes 327704
  36.4 25.1 %shard_map.101 = bf16[1024,128]{1,0:T(8,128)(2,1)} custom-call(bf16[1280,128]{1,0:T(8,128)(2,1)} %copy-done, s32[27,1024]{1,0:T(8,128)} %bitcast.10, bf16[3456,128]{1,0:T(8,128)(2,1)} %bitcast.9, bf16[128,384]{1,0:T(8,128)(2,1)} %bitcast.13, f32[1,8]{1,0:T(1,128)} %sharp_ref.1, bf16[128,128]{1,0:T(8,128)(2,1)} %bitcast.14, f32[2,128]{1,0:T(2,128)} %bitcast.15, ...), custom_call_target="tpu_custom_call" | custom-call | tf_op jit(solution)/shard_map/pallas_call | solution.py:297
Async XLA Ops:
  0.0 1.6 %copy-start.2 = (s32[1,1024]{1,0:T(1,128)S(1)}, s32[1,1024]{1,0:T(1,128)}, u32[]{:S(2)}) copy-start(s32[1,1024]{1,0:T(1,128)} %target_ref.1) | copy-start | bytes 12292
  1.6 1.0 %copy-start.1 = (bf16[1024,128]{1,0:T(8,128)(2,1)S(1)}, bf16[1024,128]{1,0:T(8,128)(2,1)}, u32[]{:S(2)}) copy-start(bf16[1024,128]{1,0:T(8,128)(2,1)} %x_ref.1) | copy-start | bytes 786436
  35.7 0.7 %copy-start = (bf16[1280,128]{1,0:T(8,128)(2,1)}, bf16[1280,128]{1,0:T(8,128)(2,1)S(1)}, u32[]{:S(2)}) copy-start(bf16[1280,128]{1,0:T(8,128)(2,1)S(1)} %shard_map.100.ext_ref) | copy-start | bytes 983044

commit v2 on v1

v2 whole, which is shorter than its diff:
```python
import functools

import jax
import jax.numpy as jnp
from jax import lax
from jax.experimental import pallas as pl
from jax.experimental.pallas import tpu as pltpu
from jax.sharding import PartitionSpec as P

MESH = pl.DeviceIdType.MESH
F32, BF16, I32 = jnp.float32, jnp.bfloat16, jnp.int32
ROWS = 1024
C = 128
HALO = 128
HEADS = 8
TAPS = 27
EXT = ROWS + 2 * HALO
BLK = 256
LOG2E = 1.4426950408889634


def dot(a, b):
    return jnp.dot(a, b, preferred_element_type=F32)


def dot_nt(a, b):
    return lax.dot_general(a, b, (((1,), (1,)), ((), ())), preferred_element_type=F32)


def onehot(mask):
    return jnp.where(mask, 1.0, 0.0).astype(BF16)


def flip(values):
    return jnp.transpose(values.astype(F32), (1, 0))


def iota(shape, dim):
    return lax.broadcasted_iota(I32, shape, dim)


def z_peer(dz):
    return (lax.axis_index("tile"), lax.axis_index("pts"), (lax.axis_index("grp") + dz) & 7)


def xy_peer(half, idx):
    me = lax.axis_index("pts")
    dy = idx >> 1
    dx = 2 * (idx & 1) + ((half + dy) & 1)
    return (
        lax.axis_index("tile"),
        (((me >> 2) + dy) & 3) * 4 + (((me & 3) + dx) & 3),
        lax.axis_index("grp"),
    )


def slab_peer(step):
    me = (lax.axis_index("pts") * 8 + lax.axis_index("grp") + step) & 127
    return (lax.axis_index("tile"), me >> 3, me & 7)


def block_kernel(
    x_hbm, target_hbm, adj_hbm, stencil_hbm, lens_hbm, sharp_ref, mixer_hbm, film_ref, wide_hbm,
    narrow_hbm, out_ref, x, target_in, adj_in, stencil_in, lens_in, mixer_in, wide_in, narrow_in,
    send, mid, land, msend, mmid, mland, rim, wants, hits, sides, ext, gathered, conv,
    stencil, lens, mixer, wide, narrow, keys, ssem, rsem, hsem, isem,
):
    pts, grp = lax.axis_index("pts"), lax.axis_index("grp")
    loads = [
        pltpu.make_async_copy(src, dst, isem.at[i])
        for i, (src, dst) in enumerate(
            (
                (target_hbm, target_in), (x_hbm, x), (adj_hbm, adj_in), (lens_hbm, lens_in),
                (mixer_hbm, mixer_in), (wide_hbm, wide_in), (narrow_hbm, narrow_in),
                (stencil_hbm, stencil_in),
            )
        )
    ]
    loads[0].start()
    loads[1].start()
    peers = [z_peer(i) for i in range(1, 8)]
    peers += [xy_peer(0, i) for i in range(1, 8)] + [xy_peer(1, i) for i in range(8)]
    peers += [slab_peer(1), slab_peer(-1)]
    barrier = pltpu.get_barrier_semaphore()
    for peer in peers:
        pl.semaphore_signal(barrier, inc=1, device_id=peer, device_id_type=MESH)
    for load in loads[2:]:
        load.start()

    loads[0].wait()
    target = target_in[...]
    owner = target >> 10
    dy = ((owner >> 5) - (pts >> 2)) & 3
    dx = ((owner >> 3) - (pts & 3)) & 3
    dz = (owner - grp) & 7
    flat = dy * 2 + (dx >> 1)
    group = jnp.where(((dx + dy) & 1) == 0, dz * 8 + flat, 64 + flat * 8 + dz)
    member = iota((128, ROWS), 0) == group
    member_bf = onehot(member)
    earlier = onehot(iota((BLK, BLK), 0) < iota((BLK, BLK), 1))
    carry = jnp.zeros((128, 1), F32)
    ranks = []
    for b in range(ROWS // BLK):
        cols = slice(b * BLK, (b + 1) * BLK)
        part = member_bf[:, cols]
        count = dot(part, earlier) + carry
        ranks.append(jnp.sum(jnp.where(member[:, cols], count, 0.0), axis=0, keepdims=True))
        if b < ROWS // BLK - 1:
            carry = carry + jnp.sum(part.astype(F32), axis=1, keepdims=True)
    rank = jnp.concatenate(ranks, axis=1).astype(I32)
    slot = group * 16 + rank
    lane = ((group >> 3) & 7) * 16 + rank
    place = (target & 1023) + 1
    here = iota((128, ROWS), 0) == lane
    high = jnp.where(here, (place >> 5).astype(F32), 0.0).astype(BF16)
    low = jnp.where(here, (place & 31).astype(F32), 0.0).astype(BF16)
    meta = (32.0 * dot_nt(member_bf, high) + dot_nt(member_bf, low)).reshape(16, 8, 128)
    msend[...] = meta
    mmid[0] = meta[0]
    loads[1].wait()

    def pack(m0):
        hit = onehot(iota((512, ROWS), 0) + m0 * 128 == slot)
        return dot(hit, x[...]).astype(BF16).reshape(4, 8, 16, C)

    packed = pack(0)
    send[0:4] = packed
    mid[0] = packed[0]

    pl.semaphore_wait(barrier, len(peers))

    def remote(kind, stage, idx, src, dst, peer):
        return pltpu.make_async_remote_copy(
            src, dst, ssem.at[kind, stage, idx], rsem.at[kind, stage, idx],
            device_id=peer, device_id_type=MESH,
        )

    def stage_copies(kind, one, two, three):
        first = [remote(kind, 0, i, one.at[i], two.at[i], z_peer(i)) for i in range(1, 8)]
        second = [remote(kind, 1, i, one.at[8 + i], two.at[8 + i], xy_peer(1, i)) for i in range(8)]
        third = [
            remote(kind, 2, i, two.at[0:8, i], three.at[i], xy_peer(0, i)) for i in range(1, 8)
        ]
        fourth = [
            remote(kind, 3, i, two.at[8:16, i], three.at[8 + i], z_peer(i)) for i in range(1, 8)
        ]
        return first, second, third, fourth

    meta_copies = stage_copies(0, msend, mmid, mland)
    data_copies = stage_copies(1, send, mid, land)

    def start(copies):
        for copy in copies:
            copy.start()

    def arrived(copies):
        for copy in copies:
            copy.wait_recv()

    start(data_copies[0][0:3])
    send[4:8] = pack(4)
    start(data_copies[0][3:7])
    for m0 in (8, 12):
        send[m0 : m0 + 4] = pack(m0)
        start(data_copies[1][m0 - 8 : m0 - 4])
    start(meta_copies[0])
    start(meta_copies[1])

    first_row = (pts * 8 + grp) * ROWS
    base = first_row - HALO + (iota((1, ROWS), 1) >> 8) * BLK

    def tap_hits(t, carry):
        adj = adj_in[t]
        rel = adj - base
        near = jnp.where(adj < 0, -1, rel & (BLK - 1))
        sides[t] = rel
        hits[t] = onehot(iota((BLK, ROWS), 0) == near)
        return carry

    loads[2].wait()
    lax.fori_loop(0, 9, tap_hits, 0)
    for load in loads[3:]:
        load.wait()
    for i in range(3):
        lens[i * C : (i + 1) * C] = flip(lens_in[:, i * C : (i + 1) * C]).astype(BF16)
    mixer[...] = flip(mixer_in[...]).astype(BF16)
    for i in range(4):
        wide[i * C : (i + 1) * C] = flip(wide_in[:, i * C : (i + 1) * C]).astype(BF16)
        narrow[:, i * C : (i + 1) * C] = flip(narrow_in[i * C : (i + 1) * C]).astype(BF16)
    for t in range(TAPS):
        stencil[:, t * C : (t + 1) * C] = flip(stencil_in[t * C : (t + 1) * C]).astype(BF16)
    film = flip(jnp.concatenate([film_ref[...], jnp.zeros((6, C), F32)], axis=0))

    arrived(data_copies[1])
    start(data_copies[3])
    arrived(meta_copies[0])
    start(meta_copies[2])
    arrived(meta_copies[1])
    start(meta_copies[3])
    mland[0] = mmid[0:8, 0]
    mland[8] = mmid[8:16, 0]
    land[8] = mid[8:16, 0]
    lax.fori_loop(9, 15, tap_hits, 0)
    arrived(data_copies[0])
    start(data_copies[2])
    land[0] = mid[0:8, 0]
    lax.fori_loop(15, TAPS, tap_hits, 0)
    arrived(meta_copies[2])
    arrived(meta_copies[3])
    places = jnp.sum(mland[...], axis=1)
    for m in range(16):
        wants[:, m * C : (m + 1) * C] = onehot(
            (iota((ROWS, C), 0) + 1).astype(F32) == places[m : m + 1]
        )
    half = ROWS
    arrived(data_copies[2])
    own = dot(wants[:, :half], land[0:8].reshape(half, C))
    arrived(data_copies[3])
    own = own + dot(wants[:, half:], land[8:16].reshape(half, C))
    rim[0] = own[:HALO].astype(BF16)
    rim[1] = own[ROWS - HALO :].astype(BF16)
    down = pltpu.make_async_remote_copy(
        rim.at[0], rim.at[2], hsem.at[0], hsem.at[1], device_id=slab_peer(-1), device_id_type=MESH
    )
    up = pltpu.make_async_remote_copy(
        rim.at[1], rim.at[3], hsem.at[2], hsem.at[3], device_id=slab_peer(1), device_id_type=MESH
    )
    down.start()
    up.start()
    ext[:, HALO : HALO + ROWS] = flip(own).astype(BF16)

    def convolve(b):
        at = pl.multiple_of(b * BLK, BLK)
        cols = pl.ds(at, BLK)
        pair = jnp.concatenate(
            [ext[:, cols], ext[:, pl.ds(pl.multiple_of(at + BLK, BLK), BLK)]], axis=0
        )
        for t in range(TAPS):
            both = dot(pair, hits[t, :, cols])
            gathered[t * C : (t + 1) * C] = jnp.where(
                sides[t, :, cols] >= BLK, both[C:], both[:C]
            ).astype(BF16)
        conv[:, cols] = dot(stencil[...], gathered[...])

    lax.fori_loop(1, 3, lambda b, c: (convolve(b), c)[1], 0)
    up.wait()
    ext[:, 0:HALO] = flip(rim[3]).astype(BF16)
    down.wait()
    ext[:, HALO + ROWS :] = flip(rim[2]).astype(BF16)
    lax.fori_loop(0, 2, lambda b, c: (convolve(3 * b), c)[1], 0)

    after_conv = ext[:, HALO : HALO + ROWS].astype(F32) + normalize(conv[...])
    conv[...] = after_conv
    normed = normalize(after_conv).astype(BF16)
    projected = dot(lens[...], normed)

    def unit(values):
        shaped = values.reshape(HEADS, C // HEADS, ROWS)
        power = jnp.mean(shaped * shaped, axis=1, keepdims=True)
        return (shaped * lax.rsqrt(jnp.maximum(power, 0.25))).reshape(C, ROWS)

    queries = unit(projected[:C]).astype(BF16)
    keys[...] = flip(unit(projected[C : 2 * C])).astype(BF16)
    values = projected[2 * C :].astype(BF16)
    ones = jnp.ones((C // HEADS, ROWS), BF16)
    head_of = iota((C, ROWS), 0) >> 4
    mixed = []
    for h in range(HEADS):
        query = jnp.where(head_of == h, queries, jnp.zeros_like(queries))
        value = jnp.concatenate([values[16 * h : 16 * h + 16], ones], axis=0)
        outs = []
        for b in range(2):
            scores = dot(keys[...], query[:, b * 512 : (b + 1) * 512])
            weights = jnp.exp2(scores * (sharp_ref[0, h] * (LOG2E / 16))).astype(BF16)
            sums = dot(value, weights)
            outs.append(sums[:16] / sums[16:])
        mixed.append(jnp.concatenate(outs, axis=1))
    mixed = jnp.concatenate(mixed, axis=0).astype(BF16)
    after_attn = conv[...] + dot(mixer[...], mixed)
    film_input = (normalize(after_attn) * (1.0 + film[:, 0:1]) + film[:, 1:2]).astype(BF16)
    hidden = jax.nn.gelu(dot(wide[...], film_input), approximate=True).astype(BF16)
    out_ref[...] = flip(after_attn + dot(narrow[...], hidden)).astype(BF16)
    for copies in meta_copies + data_copies:
        for copy in copies:
            copy.wait_send()


def normalize(values):
    average = jnp.mean(values, axis=0, keepdims=True)
    centred = values - average
    spread = jnp.mean(centred * centred, axis=0, keepdims=True)
    return centred * lax.rsqrt(spread + 1e-05)


def shards(features, targets, adjacency, stencil, lens, sharp, mixer, film, wide, narrow):
    hbm = pl.BlockSpec(memory_space=pl.ANY)
    vmem = pl.BlockSpec(memory_space=pltpu.VMEM)
    smem = pl.BlockSpec(memory_space=pltpu.SMEM)
    hid = wide.shape[-1]
    return pl.pallas_call(
        block_kernel,
        out_shape=jax.ShapeDtypeStruct((ROWS, C), BF16),
        in_specs=[hbm] * 5 + [smem, hbm, vmem, hbm, hbm],
        out_specs=vmem,
        scratch_shapes=[
            pltpu.VMEM((ROWS, C), BF16),
            pltpu.VMEM((1, ROWS), I32),
            pltpu.VMEM((TAPS, 1, ROWS), I32),
            pltpu.VMEM((TAPS * C, C), BF16),
            pltpu.VMEM((C, 3 * C), BF16),
            pltpu.VMEM((C, C), BF16),
            pltpu.VMEM((C, hid), BF16),
            pltpu.VMEM((hid, C), BF16),
        ]
        + [pltpu.VMEM((16, 8, 16, C), BF16)] * 3
        + [pltpu.VMEM((16, 8, 128), F32)] * 3
        + [
            pltpu.VMEM((4, HALO, C), BF16),
            pltpu.VMEM((ROWS, 2 * ROWS), BF16),
            pltpu.VMEM((TAPS, BLK, ROWS), BF16),
            pltpu.VMEM((TAPS, 1, ROWS), I32),
            pltpu.VMEM((C, EXT), BF16),
            pltpu.VMEM((TAPS * C, BLK), BF16),
            pltpu.VMEM((C, ROWS), F32),
            pltpu.VMEM((C, TAPS * C), BF16),
            pltpu.VMEM((3 * C, C), BF16),
            pltpu.VMEM((C, C), BF16),
            pltpu.VMEM((hid, C), BF16),
            pltpu.VMEM((C, hid), BF16),
            pltpu.VMEM((ROWS, C), BF16),
            pltpu.SemaphoreType.DMA((2, 4, 8)),
            pltpu.SemaphoreType.DMA((2, 4, 8)),
            pltpu.SemaphoreType.DMA((4,)),
            pltpu.SemaphoreType.DMA((8,)),
        ],
        compiler_params=pltpu.CompilerParams(
            collective_id=0, has_side_effects=True, vmem_limit_bytes=56 << 20
        ),
    )(
        features, targets, adjacency.reshape(TAPS, 1, ROWS), stencil.reshape(TAPS * C, C),
        lens[0], sharp, mixer[0], film.reshape(2, C), wide[0], narrow[0],
    )


def solution(mesh):
    rows = P(("tile", "pts", "grp"), None)
    in_specs = (
        rows,
        P(None, ("tile", "pts", "grp")),
        P(None, None, ("tile", "pts", "grp")),
        P(), P(), P(), P(), P("tile"), P(), P(),
    )
    return jax.shard_map(shards, mesh=mesh, in_specs=in_specs, out_specs=rows, check_vma=False)
```

time: 61.7 us -> 50.8 us (0.82)
  the two profiles are of different devices: /device:TPU:8 before, /device:TPU:1 now
where the time goes in v2:
time: 50.8 us; the launch traced here: 50.7 us
  Pallas kernels  49 us (96%)
  local copies, waits for them, and re-layouts  1.67 us (3%)
    pallas_call x1, Pallas kernels, shards(): pl.pallas_call(block_kernel, out_shape=jax.ShapeDtypeStruct((ROWS, C), BF...  49 us
    unnamed x1, local copies, waits for them, and re-layouts  1.67 us

profile of v2, /device:TPU:1, one launch (start us, length us, event | category | flops | bytes accessed | tf_op | source)
XLA Modules:
  0.0 50.7 jit_solution(12072581427873618064)
XLA Ops:
  0.0 49.0 %shard_map.100 = bf16[1024,128]{1,0:T(8,128)(2,1)} custom-call(bf16[1024,128]{1,0:T(8,128)(2,1)} %x_hbm.1, s32[1,1024]{1,0:T(1,128)} %target_hbm.1, s32[27,1,1024]{2,1,0:T(1,128)} %bitcast.10, bf16[3456,128]{1,0:T(8,128)(2,1)} %bitcast.7, bf16[128,384]{1,0:T(8,128)(2,1)} %bitcast.11, f32[1,8]{1,0:T(1,128)} %sharp_ref.1, bf16[128,128]{1,0:T(8,128)(2,1)} %bitcast.12, ...), custom_call_target="tpu_custom_call" | custom-call | tf_op jit(solution)/shard_map/pallas_call | solution.py:300
  49.0 1.7 %copy.12 = bf16[1024,128]{1,0:T(8,128)(2,1)} copy(bf16[1024,128]{1,0:T(8,128)(2,1)} %shard_map.100) | data formatting | bytes 524288

commit v3 on v2

--- a/solution.py
+++ b/solution.py
@@ -62,7 +62,7 @@
 def block_kernel(
     x_hbm, target_hbm, adj_hbm, stencil_hbm, lens_hbm, sharp_ref, mixer_hbm, film_ref, wide_hbm,
     narrow_hbm, out_ref, x, target_in, adj_in, stencil_in, lens_in, mixer_in, wide_in, narrow_in,
-    send, mid, land, msend, mmid, mland, rim, wants, hits, sides, ext, gathered, conv,
+    send, mid, land, msend, mmid, mland, wants, hits, sides, ext, gathered, conv,
     stencil, lens, mixer, wide, narrow, keys, ssem, rsem, hsem, isem,
 ):
     pts, grp = lax.axis_index("pts"), lax.axis_index("grp")
@@ -80,10 +80,16 @@
     loads[1].start()
     peers = [z_peer(i) for i in range(1, 8)]
     peers += [xy_peer(0, i) for i in range(1, 8)] + [xy_peer(1, i) for i in range(8)]
-    peers += [slab_peer(1), slab_peer(-1)]
+    slab = pts * 8 + grp
     barrier = pltpu.get_barrier_semaphore()
+
+    def greet(peer):
+        pl.semaphore_signal(barrier, inc=1, device_id=peer, device_id_type=MESH)
+
     for peer in peers:
-        pl.semaphore_signal(barrier, inc=1, device_id=peer, device_id_type=MESH)
+        greet(peer)
+    pl.when(slab > 0)(lambda: greet(slab_peer(-1)))
+    pl.when(slab < 127)(lambda: greet(slab_peer(1)))
     for load in loads[2:]:
         load.start()
 
@@ -94,7 +100,8 @@
     dx = ((owner >> 3) - (pts & 3)) & 3
     dz = (owner - grp) & 7
     flat = dy * 2 + (dx >> 1)
-    group = jnp.where(((dx + dy) & 1) == 0, dz * 8 + flat, 64 + flat * 8 + dz)
+    odd = (dx + dy) & 1
+    group = jnp.where(odd == 0, dz * 8 + flat, 64 + flat * 8 + dz)
     member = iota((128, ROWS), 0) == group
     member_bf = onehot(member)
     earlier = onehot(iota((BLK, BLK), 0) < iota((BLK, BLK), 1))
@@ -114,7 +121,8 @@
     here = iota((128, ROWS), 0) == lane
     high = jnp.where(here, (place >> 5).astype(F32), 0.0).astype(BF16)
     low = jnp.where(here, (place & 31).astype(F32), 0.0).astype(BF16)
-    meta = (32.0 * dot_nt(member_bf, high) + dot_nt(member_bf, low)).reshape(16, 8, 128)
+    by_z = onehot(iota((128, ROWS), 0) == dz * 16 + odd * 8 + flat)
+    meta = (32.0 * dot_nt(by_z, high) + dot_nt(by_z, low)).reshape(8, 16, 128)
     msend[...] = meta
     mmid[0] = meta[0]
     loads[1].wait()
@@ -127,35 +135,36 @@
     send[0:4] = packed
     mid[0] = packed[0]
 
-    pl.semaphore_wait(barrier, len(peers))
-
-    def remote(kind, stage, idx, src, dst, peer):
+    inward = jnp.minimum(slab, 1) + jnp.minimum(127 - slab, 1)
+    pl.semaphore_wait(barrier, len(peers) + inward)
+
+    def remote(stage, src, dst, peer):
         return pltpu.make_async_remote_copy(
-            src, dst, ssem.at[kind, stage, idx], rsem.at[kind, stage, idx],
-            device_id=peer, device_id_type=MESH,
+            src, dst, ssem.at[stage], rsem.at[stage], device_id=peer, device_id_type=MESH
         )
 
-    def stage_copies(kind, one, two, three):
-        first = [remote(kind, 0, i, one.at[i], two.at[i], z_peer(i)) for i in range(1, 8)]
-        second = [remote(kind, 1, i, one.at[8 + i], two.at[8 + i], xy_peer(1, i)) for i in range(8)]
-        third = [
-            remote(kind, 2, i, two.at[0:8, i], three.at[i], xy_peer(0, i)) for i in range(1, 8)
-        ]
-        fourth = [
-            remote(kind, 3, i, two.at[8:16, i], three.at[8 + i], z_peer(i)) for i in range(1, 8)
-        ]
-        return first, second, third, fourth
-
-    meta_copies = stage_copies(0, msend, mmid, mland)
-    data_copies = stage_copies(1, send, mid, land)
+    data_copies = (
+        [remote(0, send.at[i], mid.at[i], z_peer(i)) for i in range(1, 8)],
+        [remote(1, send.at[8 + i], mid.at[8 + i], xy_peer(1, i)) for i in range(8)],
+        [remote(2, mid.at[0:8, i], land.at[i], xy_peer(0, i)) for i in range(1, 8)],
+        [remote(3, mid.at[8:16, i], land.at[8 + i], z_peer(i)) for i in range(1, 8)],
+    )
+    meta_copies = (
+        [remote(4, msend.at[i], mmid.at[i], z_peer(i)) for i in range(1, 8)],
+        [
+            remote(5, mmid.at[0:8, i], mland.at[i], xy_peer(i >> 3, i & 7)) for i in range(1, 16)
+        ],
+    )
+    landed = (
+        mid.at[1:8], mid.at[8:16], land.at[1:8], land.at[9:16], mmid.at[1:8], mland.at[1:16]
+    )
 
     def start(copies):
         for copy in copies:
             copy.start()
 
-    def arrived(copies):
-        for copy in copies:
-            copy.wait_recv()
+    def arrived(stage):
+        pltpu.make_async_copy(landed[stage], landed[stage], rsem.at[stage]).wait()
 
     start(data_copies[0][0:3])
     send[4:8] = pack(4)
@@ -164,15 +173,21 @@
         send[m0 : m0 + 4] = pack(m0)
         start(data_copies[1][m0 - 8 : m0 - 4])
     start(meta_copies[0])
-    start(meta_copies[1])
-
-    first_row = (pts * 8 + grp) * ROWS
-    base = first_row - HALO + (iota((1, ROWS), 1) >> 8) * BLK
+
+    point = iota((1, ROWS), 1)
+    inner = (point >= HALO) & (point < ROWS - HALO)
+    upper = point >= ROWS - HALO
+    base = jnp.where(
+        inner, ((point - HALO) >> 8) * BLK, jnp.where(upper, ROWS - 2 * HALO, -HALO)
+    )
+    base = base + slab * ROWS
+    low_bits = jnp.where(inner, BLK - 1, HALO - 1)
+    lift = jnp.where(upper, HALO, 0)
 
     def tap_hits(t, carry):
         adj = adj_in[t]
         rel = adj - base
-        near = jnp.where(adj < 0, -1, rel & (BLK - 1))
+        near = jnp.where(adj < 0, -1, (rel & low_bits) + lift)
         sides[t] = rel
         hits[t] = onehot(iota((BLK, ROWS), 0) == near)
         return carry
@@ -191,63 +206,93 @@
         stencil[:, t * C : (t + 1) * C] = flip(stencil_in[t * C : (t + 1) * C]).astype(BF16)
     film = flip(jnp.concatenate([film_ref[...], jnp.zeros((6, C), F32)], axis=0))
 
-    arrived(data_copies[1])
+    arrived(1)
     start(data_copies[3])
-    arrived(meta_copies[0])
-    start(meta_copies[2])
-    arrived(meta_copies[1])
-    start(meta_copies[3])
+    arrived(4)
+    start(meta_copies[1])
     mland[0] = mmid[0:8, 0]
-    mland[8] = mmid[8:16, 0]
     land[8] = mid[8:16, 0]
     lax.fori_loop(9, 15, tap_hits, 0)
-    arrived(data_copies[0])
+    arrived(0)
     start(data_copies[2])
     land[0] = mid[0:8, 0]
     lax.fori_loop(15, TAPS, tap_hits, 0)
-    arrived(meta_copies[2])
-    arrived(meta_copies[3])
-    places = jnp.sum(mland[...], axis=1)
+    arrived(5)
+    places = jnp.concatenate([jnp.sum(mland[0:8], axis=1), jnp.sum(mland[8:16], axis=0)], axis=0)
+    places = flip(places)
     for m in range(16):
-        wants[:, m * C : (m + 1) * C] = onehot(
-            (iota((ROWS, C), 0) + 1).astype(F32) == places[m : m + 1]
+        wants[m * C : (m + 1) * C] = onehot(
+            (iota((C, ROWS), 1) + 1).astype(F32) == places[:, m : m + 1]
         )
-    half = ROWS
-    arrived(data_copies[2])
-    own = dot(wants[:, :half], land[0:8].reshape(half, C))
-    arrived(data_copies[3])
-    own = own + dot(wants[:, half:], land[8:16].reshape(half, C))
-    rim[0] = own[:HALO].astype(BF16)
-    rim[1] = own[ROWS - HALO :].astype(BF16)
+
+    def unpack(m0):
+        rows = [flip(land[m].reshape(C, C)).astype(BF16) for m in range(m0, m0 + 8)]
+        return dot(jnp.concatenate(rows, axis=1), wants[m0 * C : (m0 + 8) * C])
+
+    arrived(2)
+    own = unpack(0)
+    arrived(3)
+    ext[:, HALO : HALO + ROWS] = (own + unpack(8)).astype(BF16)
     down = pltpu.make_async_remote_copy(
-        rim.at[0], rim.at[2], hsem.at[0], hsem.at[1], device_id=slab_peer(-1), device_id_type=MESH
+        ext.at[:, HALO : 2 * HALO], ext.at[:, EXT - HALO : EXT], hsem.at[0], hsem.at[1],
+        device_id=slab_peer(-1), device_id_type=MESH,
     )
     up = pltpu.make_async_remote_copy(
-        rim.at[1], rim.at[3], hsem.at[2], hsem.at[3], device_id=slab_peer(1), device_id_type=MESH
-    )
-    down.start()
-    up.start()
-    ext[:, HALO : HALO + ROWS] = flip(own).astype(BF16)
-
-    def convolve(b):
-        at = pl.multiple_of(b * BLK, BLK)
-        cols = pl.ds(at, BLK)
-        pair = jnp.concatenate(
-            [ext[:, cols], ext[:, pl.ds(pl.multiple_of(at + BLK, BLK), BLK)]], axis=0
-        )
+        ext.at[:, ROWS : ROWS + HALO], ext.at[:, 0:HALO], hsem.at[2], hsem.at[3],
+        device_id=slab_peer(1), device_id_type=MESH,
+    )
+    pl.when(slab > 0)(down.start)
+    pl.when(slab < 127)(up.start)
+
+    for b in range(3):
+        at = HALO + b * BLK
+        cols = slice(at, at + BLK)
+        pair = jnp.concatenate([ext[:, at : at + BLK], ext[:, at + BLK : at + 2 * BLK]], axis=0)
         for t in range(TAPS):
             both = dot(pair, hits[t, :, cols])
-            gathered[t * C : (t + 1) * C] = jnp.where(
+            gathered[t * C : (t + 1) * C, cols] = jnp.where(
                 sides[t, :, cols] >= BLK, both[C:], both[:C]
             ).astype(BF16)
-        conv[:, cols] = dot(stencil[...], gathered[...])
-
-    lax.fori_loop(1, 3, lambda b, c: (convolve(b), c)[1], 0)
-    up.wait()
-    ext[:, 0:HALO] = flip(rim[3]).astype(BF16)
-    down.wait()
-    ext[:, HALO + ROWS :] = flip(rim[2]).astype(BF16)
-    lax.fori_loop(0, 2, lambda b, c: (convolve(3 * b), c)[1], 0)
+        conv[:, cols] = dot(stencil[...], gathered[:, cols])
+
+    @pl.when(slab > 0)
+    def _():
+        up.wait_recv()
+
+    @pl.when(slab == 0)
+    def _():
+        ext[:, 0:HALO] = jnp.zeros((C, HALO), BF16)
+
+    @pl.when(slab < 127)
+    def _():
+        down.wait_recv()
+
+    @pl.when(slab == 127)
+    def _():
+        ext[:, EXT - HALO : EXT] = jnp.zeros((C, HALO), BF16)
+
+    tail = ROWS - HALO
+    trio = jnp.concatenate(
+        [
+            jnp.concatenate(
+                [ext[:, w * HALO : (w + 1) * HALO], ext[:, tail + w * HALO : tail + (w + 1) * HALO]],
+                axis=1,
+            )
+            for w in range(3)
+        ],
+        axis=0,
+    )
+    for t in range(TAPS):
+        three = dot(trio, jnp.concatenate([hits[t, :, :HALO], hits[t, :, tail:]], axis=1))
+        side = jnp.concatenate([sides[t, :, :HALO], sides[t, :, tail:]], axis=1)
+        picked = jnp.where(
+            side >= HALO, jnp.where(side >= 2 * HALO, three[2 * C :], three[C : 2 * C]), three[:C]
+        ).astype(BF16)
+        gathered[t * C : (t + 1) * C, :HALO] = picked[:, :HALO]
+        gathered[t * C : (t + 1) * C, tail:] = picked[:, HALO:]
+    ends = dot(stencil[...], jnp.concatenate([gathered[:, :HALO], gathered[:, tail:]], axis=1))
+    conv[:, :HALO] = ends[:, :HALO]
+    conv[:, tail:] = ends[:, HALO:]
 
     after_conv = ext[:, HALO : HALO + ROWS].astype(F32) + normalize(conv[...])
     conv[...] = after_conv
@@ -280,9 +325,10 @@
     film_input = (normalize(after_attn) * (1.0 + film[:, 0:1]) + film[:, 1:2]).astype(BF16)
     hidden = jax.nn.gelu(dot(wide[...], film_input), approximate=True).astype(BF16)
     out_ref[...] = flip(after_attn + dot(narrow[...], hidden)).astype(BF16)
-    for copies in meta_copies + data_copies:
-        for copy in copies:
-            copy.wait_send()
+    for stage in range(6):
+        pltpu.make_async_copy(landed[stage], landed[stage], ssem.at[stage]).wait()
+    pl.when(slab > 0)(down.wait_send)
+    pl.when(slab < 127)(up.wait_send)
 
 
 def normalize(values):
@@ -313,14 +359,14 @@
             pltpu.VMEM((hid, C), BF16),
         ]
         + [pltpu.VMEM((16, 8, 16, C), BF16)] * 3
-        + [pltpu.VMEM((16, 8, 128), F32)] * 3
+        + [pltpu.VMEM((8, 16, 128), F32)] * 2
         + [
-            pltpu.VMEM((4, HALO, C), BF16),
-            pltpu.VMEM((ROWS, 2 * ROWS), BF16),
+            pltpu.VMEM((16, 8, 128), F32),
+            pltpu.VMEM((2 * ROWS, ROWS), BF16),
             pltpu.VMEM((TAPS, BLK, ROWS), BF16),
             pltpu.VMEM((TAPS, 1, ROWS), I32),
             pltpu.VMEM((C, EXT), BF16),
-            pltpu.VMEM((TAPS * C, BLK), BF16),
+            pltpu.VMEM((TAPS * C, ROWS), BF16),
             pltpu.VMEM((C, ROWS), F32),
             pltpu.VMEM((C, TAPS * C), BF16),
             pltpu.VMEM((3 * C, C), BF16),
@@ -328,8 +374,8 @@
             pltpu.VMEM((hid, C), BF16),
             pltpu.VMEM((C, hid), BF16),
             pltpu.VMEM((ROWS, C), BF16),
-            pltpu.SemaphoreType.DMA((2, 4, 8)),
-            pltpu.SemaphoreType.DMA((2, 4, 8)),
+            pltpu.SemaphoreType.DMA((6,)),
+            pltpu.SemaphoreType.DMA((6,)),
             pltpu.SemaphoreType.DMA((4,)),
             pltpu.SemaphoreType.DMA((8,)),
         ],

time: 50.8 us -> 46.7 us (0.919)
  the two profiles are of different devices: /device:TPU:1 before, /device:TPU:8 now
where the time goes in v3:
time: 46.7 us; the launch traced here: 45.9 us
  Pallas kernels  44.3 us (95%)
  local copies, waits for them, and re-layouts  1.67 us (4%)
    pallas_call x1, Pallas kernels, shards(): pl.pallas_call(block_kernel, out_shape=jax.ShapeDtypeStruct((ROWS, C), BF...  44.3 us
    unnamed x1, local copies, waits for them, and re-layouts  1.67 us

profile of v3, /device:TPU:8, one launch (start us, length us, event | category | flops | bytes accessed | tf_op | source)
XLA Modules:
  0.0 45.9 jit_solution(17359630214434583478)
XLA Ops:
  0.0 44.3 %shard_map.100 = bf16[1024,128]{1,0:T(8,128)(2,1)} custom-call(bf16[1024,128]{1,0:T(8,128)(2,1)} %x_hbm.1, s32[1,1024]{1,0:T(1,128)} %target_hbm.1, s32[27,1,1024]{2,1,0:T(1,128)} %bitcast.10, bf16[3456,128]{1,0:T(8,128)(2,1)} %bitcast.7, bf16[128,384]{1,0:T(8,128)(2,1)} %bitcast.11, f32[1,8]{1,0:T(1,128)} %sharp_ref.1, bf16[128,128]{1,0:T(8,128)(2,1)} %bitcast.12, ...), custom_call_target="tpu_custom_call" | custom-call | tf_op jit(solution)/shard_map/pallas_call | solution.py:346
  44.3 1.7 %copy.12 = bf16[1024,128]{1,0:T(8,128)(2,1)} copy(bf16[1024,128]{1,0:T(8,128)(2,1)} %shard_map.100) | data formatting | bytes 524288

commit v4 on v3

--- a/solution.py
+++ b/solution.py
@@ -116,6 +116,53 @@
             carry = carry + jnp.sum(part.astype(F32), axis=1, keepdims=True)
     rank = jnp.concatenate(ranks, axis=1).astype(I32)
     slot = group * 16 + rank
+    loads[1].wait()
+
+    def pack(m0):
+        hit = onehot(iota((512, ROWS), 0) + m0 * 128 == slot)
+        return dot(hit, x[...]).astype(BF16).reshape(4, 8, 16, C)
+
+    packed = pack(0)
+    send[0:4] = packed
+    mid[0] = packed[0]
+
+    inward = jnp.minimum(slab, 1) + jnp.minimum(127 - slab, 1)
+    pl.semaphore_wait(barrier, len(peers) + inward)
+
+    def remote(stage, src, dst, peer):
+        return pltpu.make_async_remote_copy(
+            src, dst, ssem.at[stage], rsem.at[stage], device_id=peer, device_id_type=MESH
+        )
+
+    data_copies = (
+        [remote(0, send.at[i], mid.at[i], z_peer(i)) for i in range(1, 8)],
+        [remote(1, send.at[8 + i], mid.at[8 + i], xy_peer(1, i)) for i in range(8)],
+        [remote(2, mid.at[0:8, i], land.at[i], xy_peer(0, i)) for i in range(1, 8)],
+        [remote(3, mid.at[8:16, i], land.at[8 + i], z_peer(i)) for i in range(1, 8)],
+    )
+    meta_copies = (
+        [remote(4, msend.at[i], mmid.at[i], z_peer(i)) for i in range(1, 8)],
+        [
+            remote(5, mmid.at[0:8, i], mland.at[i], xy_peer(i >> 3, i & 7)) for i in range(1, 16)
+        ],
+    )
+    landed = (
+        mid.at[1:8], mid.at[8:16], land.at[1:8], land.at[9:16], mmid.at[1:8], mland.at[1:16]
+    )
+
+    def start(copies):
+        for copy in copies:
+            copy.start()
+
+    def arrived(stage):
+        pltpu.make_async_copy(landed[stage], landed[stage], rsem.at[stage]).wait()
+
+    start(data_copies[0][0:3])
+    send[4:8] = pack(4)
+    start(data_copies[0][3:7])
+    for m0 in (8, 12):
+        send[m0 : m0 + 4] = pack(m0)
+        start(data_copies[1][m0 - 8 : m0 - 4])
     lane = ((group >> 3) & 7) * 16 + rank
     place = (target & 1023) + 1
     here = iota((128, ROWS), 0) == lane
@@ -125,53 +172,6 @@
     meta = (32.0 * dot_nt(by_z, high) + dot_nt(by_z, low)).reshape(8, 16, 128)
     msend[...] = meta
     mmid[0] = meta[0]
-    loads[1].wait()
-
-    def pack(m0):
-        hit = onehot(iota((512, ROWS), 0) + m0 * 128 == slot)
-        return dot(hit, x[...]).astype(BF16).reshape(4, 8, 16, C)
-
-    packed = pack(0)
-    send[0:4] = packed
-    mid[0] = packed[0]
-
-    inward = jnp.minimum(slab, 1) + jnp.minimum(127 - slab, 1)
-    pl.semaphore_wait(barrier, len(peers) + inward)
-
-    def remote(stage, src, dst, peer):
-        return pltpu.make_async_remote_copy(
-            src, dst, ssem.at[stage], rsem.at[stage], device_id=peer, device_id_type=MESH
-        )
-
-    data_copies = (
-        [remote(0, send.at[i], mid.at[i], z_peer(i)) for i in range(1, 8)],
-        [remote(1, send.at[8 + i], mid.at[8 + i], xy_peer(1, i)) for i in range(8)],
-        [remote(2, mid.at[0:8, i], land.at[i], xy_peer(0, i)) for i in range(1, 8)],
-        [remote(3, mid.at[8:16, i], land.at[8 + i], z_peer(i)) for i in range(1, 8)],
-    )
-    meta_copies = (
-        [remote(4, msend.at[i], mmid.at[i], z_peer(i)) for i in range(1, 8)],
-        [
-            remote(5, mmid.at[0:8, i], mland.at[i], xy_peer(i >> 3, i & 7)) for i in range(1, 16)
-        ],
-    )
-    landed = (
-        mid.at[1:8], mid.at[8:16], land.at[1:8], land.at[9:16], mmid.at[1:8], mland.at[1:16]
-    )
-
-    def start(copies):
-        for copy in copies:
-            copy.start()
-
-    def arrived(stage):
-        pltpu.make_async_copy(landed[stage], landed[stage], rsem.at[stage]).wait()
-
-    start(data_copies[0][0:3])
-    send[4:8] = pack(4)
-    start(data_copies[0][3:7])
-    for m0 in (8, 12):
-        send[m0 : m0 + 4] = pack(m0)
-        start(data_copies[1][m0 - 8 : m0 - 4])
     start(meta_copies[0])
 
     point = iota((1, ROWS), 1)
@@ -309,18 +309,24 @@
     values = projected[2 * C :].astype(BF16)
     ones = jnp.ones((C // HEADS, ROWS), BF16)
     head_of = iota((C, ROWS), 0) >> 4
-    mixed = []
+    outs = [[] for _ in range(HEADS)]
+    waiting = []
+
+    def combine():
+        h, weights = waiting.pop(0)
+        value = jnp.concatenate([values[16 * h : 16 * h + 16], ones], axis=0)
+        sums = dot(value, weights)
+        outs[h].append(sums[:16] / sums[16:])
+
     for h in range(HEADS):
         query = jnp.where(head_of == h, queries, jnp.zeros_like(queries))
-        value = jnp.concatenate([values[16 * h : 16 * h + 16], ones], axis=0)
-        outs = []
-        for b in range(2):
-            scores = dot(keys[...], query[:, b * 512 : (b + 1) * 512])
-            weights = jnp.exp2(scores * (sharp_ref[0, h] * (LOG2E / 16))).astype(BF16)
-            sums = dot(value, weights)
-            outs.append(sums[:16] / sums[16:])
-        mixed.append(jnp.concatenate(outs, axis=1))
-    mixed = jnp.concatenate(mixed, axis=0).astype(BF16)
+        for b in range(ROWS // BLK):
+            scores = dot(keys[...], query[:, b * BLK : (b + 1) * BLK])
+            waiting.append((h, jnp.exp2(scores * (sharp_ref[0, h] * (LOG2E / 16))).astype(BF16)))
+            if len(waiting) > 1:
+                combine()
+    combine()
+    mixed = jnp.concatenate([jnp.concatenate(parts, axis=1) for parts in outs], axis=0).astype(BF16)
     after_attn = conv[...] + dot(mixer[...], mixed)
     film_input = (normalize(after_attn) * (1.0 + film[:, 0:1]) + film[:, 1:2]).astype(BF16)
     hidden = jax.nn.gelu(dot(wide[...], film_input), approximate=True).astype(BF16)

time: 46.7 us -> 46.2 us (0.989); the launches traced: 45.9 us -> 46 us
  no operation moved by 1% of the time
where the time goes in v4:
time: 46.2 us; the launch traced here: 46 us
  Pallas kernels  44.3 us (96%)
  local copies, waits for them, and re-layouts  1.67 us (4%)
    pallas_call x1, Pallas kernels, shards(): pl.pallas_call(block_kernel, out_shape=jax.ShapeDtypeStruct((ROWS, C), BF...  44.3 us
    unnamed x1, local copies, waits for them, and re-layouts  1.67 us

profile of v4, /device:TPU:8, one launch (start us, length us, event | category | flops | bytes accessed | tf_op | source)
XLA Modules:
  0.0 46.0 jit_solution(18251007889686315760)
XLA Ops:
  0.0 44.3 %shard_map.100 = bf16[1024,128]{1,0:T(8,128)(2,1)} custom-call(bf16[1024,128]{1,0:T(8,128)(2,1)} %x_hbm.1, s32[1,1024]{1,0:T(1,128)} %target_hbm.1, s32[27,1,1024]{2,1,0:T(1,128)} %bitcast.10, bf16[3456,128]{1,0:T(8,128)(2,1)} %bitcast.7, bf16[128,384]{1,0:T(8,128)(2,1)} %bitcast.11, f32[1,8]{1,0:T(1,128)} %sharp_ref.1, bf16[128,128]{1,0:T(8,128)(2,1)} %bitcast.12, ...), custom_call_target="tpu_custom_call" | custom-call | tf_op jit(solution)/shard_map/pallas_call | solution.py:352
  44.4 1.7 %copy.12 = bf16[1024,128]{1,0:T(8,128)(2,1)} copy(bf16[1024,128]{1,0:T(8,128)(2,1)} %shard_map.100) | data formatting | bytes 524288

commit v5 on v4

--- a/solution.py
+++ b/solution.py
@@ -225,14 +225,24 @@
             (iota((C, ROWS), 1) + 1).astype(F32) == places[:, m : m + 1]
         )
 
-    def unpack(m0):
+    tail = ROWS - HALO
+
+    def turned(m0):
         rows = [flip(land[m].reshape(C, C)).astype(BF16) for m in range(m0, m0 + 8)]
-        return dot(jnp.concatenate(rows, axis=1), wants[m0 * C : (m0 + 8) * C])
+        return jnp.concatenate(rows, axis=1)
+
+    def unpack(rows, m0):
+        half = wants[m0 * C : (m0 + 8) * C]
+        rim = jnp.concatenate([half[:, :HALO], half[:, tail:]], axis=1)
+        return dot(rows, rim), dot(rows, half[:, HALO:tail])
 
     arrived(2)
-    own = unpack(0)
+    rim, inside = unpack(turned(0), 0)
     arrived(3)
-    ext[:, HALO : HALO + ROWS] = (own + unpack(8)).astype(BF16)
+    more_rim, more_inside = unpack(turned(8), 8)
+    rim = (rim + more_rim).astype(BF16)
+    ext[:, HALO : 2 * HALO] = rim[:, :HALO]
+    ext[:, ROWS : ROWS + HALO] = rim[:, HALO:]
     down = pltpu.make_async_remote_copy(
         ext.at[:, HALO : 2 * HALO], ext.at[:, EXT - HALO : EXT], hsem.at[0], hsem.at[1],
         device_id=slab_peer(-1), device_id_type=MESH,
@@ -243,6 +253,7 @@
     )
     pl.when(slab > 0)(down.start)
     pl.when(slab < 127)(up.start)
+    ext[:, 2 * HALO : ROWS] = (inside + more_inside).astype(BF16)
 
     for b in range(3):
         at = HALO + b * BLK
@@ -271,7 +282,6 @@
     def _():
         ext[:, EXT - HALO : EXT] = jnp.zeros((C, HALO), BF16)
 
-    tail = ROWS - HALO
     trio = jnp.concatenate(
         [
             jnp.concatenate(

time: 46.2 us -> 46 us (level)
  no operation moved by 1% of the time
where the time goes in v5:
time: 46 us; the launch traced here: 45.9 us
  Pallas kernels  44.2 us (96%)
  local copies, waits for them, and re-layouts  1.67 us (4%)
    pallas_call x1, Pallas kernels, shards(): pl.pallas_call(block_kernel, out_shape=jax.ShapeDtypeStruct((ROWS, C), BF...  44.2 us
    unnamed x1, local copies, waits for them, and re-layouts  1.67 us

profile of v5, /device:TPU:8, one launch (start us, length us, event | category | flops | bytes accessed | tf_op | source)
XLA Modules:
  0.0 45.9 jit_solution(7129153445122699429)
XLA Ops:
  0.0 44.2 %shard_map.100 = bf16[1024,128]{1,0:T(8,128)(2,1)} custom-call(bf16[1024,128]{1,0:T(8,128)(2,1)} %x_hbm.1, s32[1,1024]{1,0:T(1,128)} %target_hbm.1, s32[27,1,1024]{2,1,0:T(1,128)} %bitcast.10, bf16[3456,128]{1,0:T(8,128)(2,1)} %bitcast.7, bf16[128,384]{1,0:T(8,128)(2,1)} %bitcast.11, f32[1,8]{1,0:T(1,128)} %sharp_ref.1, bf16[128,128]{1,0:T(8,128)(2,1)} %bitcast.12, ...), custom_call_target="tpu_custom_call" | custom-call | tf_op jit(solution)/shard_map/pallas_call | solution.py:362
  44.2 1.7 %copy.12 = bf16[1024,128]{1,0:T(8,128)(2,1)} copy(bf16[1024,128]{1,0:T(8,128)(2,1)} %shard_map.100) | data formatting | bytes 524288
